TPU v7x, 256 devices: a whole 4x4x8 slice. The times are simulated.
256 devices in a mesh: grp: 4 (over y), ep: 64 (over x, z, core).
Axes of the slice: x: 4, y: 4, z: 8, core: 2. Of those that a mesh axis runs over, the one named last changes fastest.
Arguments:
- layer_input: bfloat16 [65536, 8192], P(('grp', 'ep')), may hold values from -6 to 6
- output_grad: bfloat16 [65536, 8192], P(('grp', 'ep')), may hold values from -0.119628906 to 0.119628906
- adapter_ids: int32 [65536, 1], P(('grp', 'ep')), may hold values from 0 to 63; in each aligned block of 256 rows (0 to 255, 256 to 511, ...) at most 8 rows name the same one
- owner_map: int32 [64], replicated, may hold values from 0 to 63, each once
- weights: bfloat16 [64, 2, 64, 8192], P('ep', None, None, 'grp'), may hold values from -0.0625 to 0.0625
- moment: float32 [64, 2, 64, 8192], P('ep', None, None, 'grp'), may hold values from -1.8 to 1.8
- second: float32 [64, 2, 64, 8192], P('ep', None, None, 'grp'), may hold values from 0.0002 to 0.004
Outputs:
- moment_next: float32 [64, 2, 64, 8192], P('ep', None, None, 'grp')
- second_next: float32 [64, 2, 64, 8192], P('ep', None, None, 'grp')
- direction: float32 [64, 2, 64, 8192], P('ep', None, None, 'grp')
Inputs may be any that keep to these rules, and one draw needn't show every extreme that they name: `adapter_ids`: among the rows of one device no adapter appears more than 8 times, and some adapter appears exactly 8 times. `owner_map`: each owner index appears once.
All inputs are finite; a program needn't handle non-finite values.
Results may differ from a plain program's by a relative error of at most 0.0026.
Values may be sent and summed in bfloat16 or wider, within the bound.
A program may use at most 128 MiB of HBM per device.

v0:
```python
import jax
import jax.numpy as jnp
from jax import lax
from jax.sharding import PartitionSpec as P

STEP = 100
ADAPTER_SCALING = 2.0
BETA_FIRST = 0.9
BETA_SECOND = 0.999
ADAM_EPSILON = 1e-08


def pack_slots(values, matcher, owner_count, capacity):
    packed = jnp.dot(matcher, values, preferred_element_type=jnp.float32).astype(jnp.bfloat16)
    return packed.reshape(owner_count, capacity, values.shape[1])


def outer_sums(reduced_input, reduced_gradient, input_rows, incoming_gradients):
    down_gradient = lax.dot_general(
        reduced_gradient, input_rows, (((0,), (0,)), ((), ())), preferred_element_type=jnp.float32
    )
    up_gradient = lax.dot_general(
        reduced_input,
        incoming_gradients,
        (((0,), (0,)), ((), ())),
        preferred_element_type=jnp.float32,
    )
    return ADAPTER_SCALING * jnp.stack([down_gradient, up_gradient])


def adam_step(grads, moment, second):
    moment_next = BETA_FIRST * moment + (1.0 - BETA_FIRST) * grads
    second_next = BETA_SECOND * second + (1.0 - BETA_SECOND) * grads * grads
    first_fix = 1.0 - BETA_FIRST**STEP
    second_fix = 1.0 - BETA_SECOND**STEP
    direction = moment_next / first_fix / (jnp.sqrt(second_next / second_fix) + ADAM_EPSILON)
    return (moment_next, second_next, direction)


def per_device(layer_input, output_grad, adapter_ids, owner_map, weights, moment, second):
    owner_count = lax.axis_size("ep")
    row_count = layer_input.shape[0]
    width = layer_input.shape[1]
    capacity = 2 * row_count // owner_count
    adapter_hot = (adapter_ids == jnp.arange(owner_map.shape[0], dtype=jnp.int32)[None, :]).astype(
        jnp.int32
    )
    owner_of = jnp.sum(adapter_hot * owner_map[None, :], axis=1)
    owner_hot = (owner_of[:, None] == jnp.arange(owner_count, dtype=jnp.int32)[None, :]).astype(
        jnp.int32
    )
    position = jnp.sum((jnp.cumsum(owner_hot, axis=0) - 1) * owner_hot, axis=1)
    slot_index = owner_of * capacity + position
    matcher = (
        jnp.arange(owner_count * capacity, dtype=jnp.int32)[:, None] == slot_index[None, :]
    ).astype(jnp.bfloat16)
    input_slots = pack_slots(layer_input, matcher, owner_count, capacity)
    grad_slots = pack_slots(output_grad, matcher, owner_count, capacity)
    recv_input, recv_grad = (
        lax.all_to_all(input_slots, "ep", split_axis=0, concat_axis=0, tiled=True),
        lax.all_to_all(grad_slots, "ep", split_axis=0, concat_axis=0, tiled=True),
    )
    whole = lax.all_gather(weights, "grp", axis=3, tiled=True)
    recv_input = recv_input.reshape(-1, width)
    recv_grad = recv_grad.reshape(-1, width)
    reduced_input = jnp.dot(recv_input, whole[0, 0].T, preferred_element_type=jnp.float32).astype(
        jnp.bfloat16
    )
    reduced_gradient = jnp.dot(recv_grad, whole[0, 1].T, preferred_element_type=jnp.float32).astype(
        jnp.bfloat16
    )
    partial_grads = outer_sums(reduced_input, reduced_gradient, recv_input, recv_grad)
    grads = lax.psum_scatter(partial_grads[None], "grp", scatter_dimension=3, tiled=True)
    return adam_step(grads, moment, second)


def solution(mesh):
    placed = (
        P(("grp", "ep"), None),
        P(("grp", "ep"), None),
        P(("grp", "ep"), None),
        P(),
        P("ep", None, None, "grp"),
        P("ep", None, None, "grp"),
        P("ep", None, None, "grp"),
    )
    return jax.shard_map(
        per_device,
        mesh=mesh,
        in_specs=placed,
        out_specs=(
            P("ep", None, None, "grp"),
            P("ep", None, None, "grp"),
            P("ep", None, None, "grp"),
        ),
        check_vma=False,
    )
```

profile of v0, /device:TPU:1, one launch (start us, length us, event | category | flops | bytes accessed | tf_op | source)
XLA Modules:
  0.0 493.1 jit_solution(13080129072405434227)
XLA Ops:
  7.2 0.8 select_reduce_fusion
  8.0 0.6 reduce-window.6
  8.6 0.2 slice_reduce_fusion
  8.8 0.1 fusion.22
  8.9 7.7 %fusion = bf16[64,8,8192]{2,1,0:T(8,128)(2,1)} fusion(bf16[256,8192]{1,0:T(8,128)(2,1)} %param.8, s32[256]{0:T(256)S(1)} %multiply_add_fusion.1), kind=kOutput, calls=%fused_computation.2 | convolution fusion | flops 2151809024 | bytes 12583936 | tf_op jit(solution)/shard_map/dot_general | solution.py:14
  16.7 13.2 %all-to-all-start = ((bf16[64,8,8192]{2,1,0:T(8,128)(2,1)}), bf16[64,8,8192]{2,1,0:T(8,128)(2,1)}, u32[]{:S(2)}, u32[]{:S(2)}) async-start(bf16[64,8,8192]{2,1,0:T(8,128)(2,1)} %fusion), calls=%async_computation | async-start | bytes 16777216 | tf_op jit(solution)/shard_map/all_to_all | solution.py:61
  29.8 7.7 %fusion.1 = bf16[64,8,8192]{2,1,0:T(8,128)(2,1)} fusion(bf16[256,8192]{1,0:T(8,128)(2,1)} %param.7, s32[256]{0:T(256)S(1)} %multiply_add_fusion.1), kind=kOutput, calls=%fused_computation.3 | convolution fusion | flops 2151809024 | bytes 12583936 | tf_op jit(solution)/shard_map/dot_general | solution.py:14
  37.6 178.0 %all-to-all-done = bf16[64,8,8192]{2,1,0:T(8,128)(2,1)} async-done(((bf16[64,8,8192]{2,1,0:T(8,128)(2,1)}), bf16[64,8,8192]{2,1,0:T(8,128)(2,1)}, u32[]{:S(2)}, u32[]{:S(2)}) %all-to-all-start) | async-done | bytes 8388640 | tf_op jit(solution)/shard_map/all_to_all | solution.py:61
  215.6 6.1 %all-to-all-start.1 = ((bf16[64,8,8192]{2,1,0:T(8,128)(2,1)}), bf16[64,8,8192]{2,1,0:T(8,128)(2,1)}, u32[]{:S(2)}, u32[]{:S(2)}) async-start(bf16[64,8,8192]{2,1,0:T(8,128)(2,1)} %fusion.1), calls=%async_computation.1 | async-start | bytes 16777216 | tf_op jit(solution)/shard_map/all_to_all | solution.py:60
  221.7 0.0 all-gather.2.cloned.1.call-start
  221.8 0.7 all-gather.2.cloned.1.call-update
  222.4 0.2 reduce-scatter.2.cloned.1.call-start
  222.7 36.3 %all-gather.2.cloned.1.call-done = bf16[1,2,64,8192]{3,2,1,0:T(8,128)(2,1)} async-done(((bf16[1,2,64,2048]{3,2,1,0:T(8,128)(2,1)}), bf16[1,2,64,8192]{3,2,1,0:T(8,128)(2,1)}) %all-gather.2.cloned.1.call-update) | async-done | bytes 2097168 | tf_op jit(solution)/shard_map/all_gather | solution.py:63
  258.9 148.5 %all-to-all-done.1 = bf16[64,8,8192]{2,1,0:T(8,128)(2,1)} async-done(((bf16[64,8,8192]{2,1,0:T(8,128)(2,1)}), bf16[64,8,8192]{2,1,0:T(8,128)(2,1)}, u32[]{:S(2)}, u32[]{:S(2)}) %all-to-all-start.1) | async-done | bytes 8388640 | tf_op jit(solution)/shard_map/all_to_all | solution.py:60
  407.5 11.9 %convolution_bitcast_fusion.1 = f32[1,1,64,8192]{3,2,1,0:T(8,128)S(1)} fusion(bf16[64,8,8192]{2,1,0:T(8,128)(2,1)} %all-to-all-done.1, bf16[64,8,8192]{2,1,0:T(8,128)(2,1)} %all-to-all-done, bf16[1,2,64,8192]{3,2,1,0:T(8,128)(2,1)} %all-gather.2.cloned.1.call-done), kind=kOutput, calls=%fused_computation.5 | convolution fusion | flops 1073774592 | bytes 19922944 | tf_op jit(solution)/shard_map/dot_general | solution.py:19
  419.4 13.3 %convolution_bitcast_fusion = f32[1,1,64,8192]{3,2,1,0:T(8,128)} fusion(bf16[64,8,8192]{2,1,0:T(8,128)(2,1)} %all-to-all-done, bf16[64,8,8192]{2,1,0:T(8,128)(2,1)} %all-to-all-done.1, bf16[1,2,64,8192]{3,2,1,0:T(8,128)(2,1)} %all-gather.2.cloned.1.call-done), kind=kOutput, calls=%fused_computation.4 | convolution fusion | flops 1073774592 | bytes 19922944 | tf_op jit(solution)/shard_map/dot_general | solution.py:22
  432.7 3.9 maximum_multiply_fusion
  436.6 0.0 copy-start
  436.6 0.0 copy-start.1
  436.6 0.0 reduce-scatter.2.cloned.1.call-update
  436.6 46.3 %reduce-scatter.2.cloned.1.call-done = f32[1,2,64,2048]{3,2,1,0:T(8,128)} async-done(((f32[1,2,64,8192]{3,2,1,0:T(8,128)}), f32[1,2,64,2048]{3,2,1,0:T(8,128)}) %reduce-scatter.2.cloned.1.call-update) | async-done | bytes 1048592 | tf_op jit(solution)/shard_map/reduce_scatter | solution.py:73
  483.0 0.0 copy-done
  483.0 0.0 copy-done.1
  483.0 3.3 add_divide_fusion
  (4 shorter events, 0.1 us)
Async XLA Ops:
  16.7 199.0 %all-to-all-start = ((bf16[64,8,8192]{2,1,0:T(8,128)(2,1)}), bf16[64,8,8192]{2,1,0:T(8,128)(2,1)}, u32[]{:S(2)}, u32[]{:S(2)}) async-start(bf16[64,8,8192]{2,1,0:T(8,128)(2,1)} %fusion), calls=%async_computation | async-start | bytes 16777216 | tf_op jit(solution)/shard_map/all_to_all | solution.py:61
  215.6 191.9 %all-to-all-start.1 = ((bf16[64,8,8192]{2,1,0:T(8,128)(2,1)}), bf16[64,8,8192]{2,1,0:T(8,128)(2,1)}, u32[]{:S(2)}, u32[]{:S(2)}) async-start(bf16[64,8,8192]{2,1,0:T(8,128)(2,1)} %fusion.1), calls=%async_computation.1 | async-start | bytes 16777216 | tf_op jit(solution)/shard_map/all_to_all | solution.py:60
  221.7 37.2 %all-gather.2.cloned.1.call-start = ((), (), s32[]{:S(2)}) async-start(), calls=%async_computation.3 | async-start | bytes 2621440 | tf_op jit(solution)/shard_map/all_gather | solution.py:63
  222.4 260.5 %reduce-scatter.2.cloned.1.call-start = ((), (), s32[]{:S(2)}) async-start(), calls=%async_computation.4 | async-start | bytes 5242880 | tf_op jit(solution)/shard_map/reduce_scatter | solution.py:73
  436.6 46.3 %copy-start = (f32[1,2,64,2048]{3,2,1,0:T(8,128)S(1)}, f32[1,2,64,2048]{3,2,1,0:T(8,128)}, u32[]{:S(2)}) copy-start(f32[1,2,64,2048]{3,2,1,0:T(8,128)} %param.13) | copy-start | bytes 3145732
  436.6 46.3 %copy-start.1 = (f32[1,2,64,2048]{3,2,1,0:T(8,128)S(1)}, f32[1,2,64,2048]{3,2,1,0:T(8,128)}, u32[]{:S(2)}) copy-start(f32[1,2,64,2048]{3,2,1,0:T(8,128)} %param.12) | copy-start | bytes 3145732
Sparse Core Ops, SparseCore 0:
  224.4 34.5 all-gather.1
  436.8 46.1 reduce-scatter.1
where the time goes:
time: 493 us
  waiting for transfers between devices  410 us (83%)
  matrix products  40.7 us (8%)
  starting transfers between devices  19.5 us (4%)
  between operations  14.1 us (3%)
  other arithmetic  8.74 us (2%)
    all_to_all x1, waiting for transfers between devices, per_device(): lax.all_to_all(grad_slots, 'ep', split_axis=0, concat_axis=0, tiled=True)  178 us
    all_to_all x1, waiting for transfers between devices, per_device(): lax.all_to_all(input_slots, 'ep', split_axis=0, concat_axis=0, tiled=True)  149 us
    reduce_scatter x1, waiting for transfers between devices, per_device(): lax.psum_scatter(partial_grads[None], 'grp', scatter_dimension=3, tiled=T...  46.3 us
    all_gather x1, waiting for transfers between devices, per_device(): whole = lax.all_gather(weights, 'grp', axis=3, tiled=True)  36.3 us
    dot_general x2, matrix products, pack_slots(): jnp.dot(matcher, values, preferred_element_type=jnp.float32)  15.5 us
    dot_general x1, matrix products, outer_sums(): lax.dot_general(reduced_input, incoming_gradients, (((0,), (0,)), ((), ()...  13.3 us
    all_to_all x1, starting transfers between devices, per_device(): lax.all_to_all(grad_slots, 'ep', split_axis=0, concat_axis=0, tiled=True)  13.2 us
    dot_general x1, matrix products, outer_sums(): lax.dot_general(reduced_gradient, input_rows, (((0,), (0,)), ((), ())), p...  11.9 us
  transfers between devices with their start and end apart: 4, of which 4 were waited for; matrix products, arithmetic and copies ran while one was open for 2% of the time, Pallas kernels for 0%

commit v1 on v0

--- a/solution.py
+++ b/solution.py
@@ -60,7 +60,9 @@
         lax.all_to_all(input_slots, "ep", split_axis=0, concat_axis=0, tiled=True),
         lax.all_to_all(grad_slots, "ep", split_axis=0, concat_axis=0, tiled=True),
     )
-    whole = lax.all_gather(weights, "grp", axis=3, tiled=True)
+    whole = jnp.concatenate(
+        lax.all_to_all(jnp.stack([weights] * lax.axis_size("grp")), "grp", 0, 0), axis=3
+    )
     recv_input = recv_input.reshape(-1, width)
     recv_grad = recv_grad.reshape(-1, width)
     reduced_input = jnp.dot(recv_input, whole[0, 0].T, preferred_element_type=jnp.float32).astype(

time: 493 us -> 515 us (1.045)
  waiting for transfers between devices: 410 us -> 422 us
  starting transfers between devices: 19.5 us -> 25.7 us
  local copies, waits for them, and re-layouts: 0.2 us -> 5.99 us
    all_gather x1 -> x0, waiting for transfers between devices: 36.3 us -> none  [per_device(): whole = lax.all_gather(weights, 'grp', axis=3, tiled=True)]
    all_to_all x1, waiting for transfers between devices: 149 us -> 184 us  [per_device(): lax.all_to_all(input_slots, 'ep', split_axis=0, concat_axis=0, tiled=True)]
    all_to_all x0 -> x1, waiting for transfers between devices: none -> 15.7 us  [per_device(): lax.all_to_all(jnp.stack([weights] * lax.axis_size('grp')), 'grp', 0, 0)]
  transfers between devices with their start and end apart: 4 -> 4, of which waited for: 4 -> 4; matrix products, arithmetic and copies ran while one was open for 2% -> 4% of each run, Pallas kernels for 0% -> 0%
where the time goes in v1:
time: 515 us; the launch traced here: 514 us
  waiting for transfers between devices  422 us (82%)
  matrix products  38.1 us (7%)
  starting transfers between devices  25.7 us (5%)
  between operations  14.1 us (3%)
  other arithmetic  8.69 us (2%)
  local copies, waits for them, and re-layouts  5.99 us (1%)
    all_to_all x1, waiting for transfers between devices, per_device(): lax.all_to_all(input_slots, 'ep', split_axis=0, concat_axis=0, tiled=True)  184 us
    all_to_all x1, waiting for transfers between devices, per_device(): lax.all_to_all(grad_slots, 'ep', split_axis=0, concat_axis=0, tiled=True)  178 us
    reduce_scatter x1, waiting for transfers between devices, per_device(): lax.psum_scatter(partial_grads[None], 'grp', scatter_dimension=3, tiled=T...  44.3 us
    all_to_all x1, waiting for transfers between devices, per_device(): lax.all_to_all(jnp.stack([weights] * lax.axis_size('grp')), 'grp', 0, 0)  15.7 us
    dot_general x2, matrix products, pack_slots(): jnp.dot(matcher, values, preferred_element_type=jnp.float32)  15.5 us
    all_to_all x1, starting transfers between devices, per_device(): lax.all_to_all(grad_slots, 'ep', split_axis=0, concat_axis=0, tiled=True)  14.4 us
    dot_general x1, matrix products, outer_sums(): lax.dot_general(reduced_input, incoming_gradients, (((0,), (0,)), ((), ()...  11.3 us
    dot_general x1, matrix products, outer_sums(): lax.dot_general(reduced_gradient, input_rows, (((0,), (0,)), ((), ())), p...  11.3 us
  transfers between devices with their start and end apart: 4, of which 4 were waited for; matrix products, arithmetic and copies ran while one was open for 4% of the time, Pallas kernels for 0%

profile of v1, /device:TPU:1, one launch (start us, length us, event | category | flops | bytes accessed | tf_op | source)
XLA Modules:
  0.0 514.4 jit_solution(14094456652540194357)
XLA Ops:
  7.2 0.0 copy-start.3
  7.2 0.0 copy-start.4
  7.2 2.7 stack.16
  9.8 5.0 all-to-all-start.1
  14.9 0.0 copy-done.3
  14.9 0.0 copy-done.4
  14.9 0.1 select_reduce_fusion
  15.0 0.6 reduce-window.6
  15.6 0.2 slice_reduce_fusion
  15.8 0.1 fusion.22
  15.9 7.7 %fusion = bf16[64,8,8192]{2,1,0:T(8,128)(2,1)} fusion(bf16[256,8192]{1,0:T(8,128)(2,1)} %param.8, s32[256]{0:T(256)S(1)} %multiply_add_fusion.1), kind=kOutput, calls=%fused_computation.2 | convolution fusion | flops 2151809024 | bytes 12583936 | tf_op jit(solution)/shard_map/dot_general | solution.py:14
  23.7 15.7 %all-to-all-done.1 = bf16[4,1,2,64,2048]{4,3,2,1,0:T(8,128)(2,1)S(1)} async-done(((bf16[4,1,2,64,2048]{4,3,2,1,0:T(8,128)(2,1)}), bf16[4,1,2,64,2048]{4,3,2,1,0:T(8,128)(2,1)S(1)}, u32[]{:S(2)}, u32[]{:S(2)}) %all-to-all-start.1) | async-done | bytes 2097184 | tf_op jit(solution)/shard_map/all_to_all | solution.py:64
  39.4 0.0 copy-start
  39.4 1.4 copy-done
  40.8 14.4 %all-to-all-start = ((bf16[64,8,8192]{2,1,0:T(8,128)(2,1)}), bf16[64,8,8192]{2,1,0:T(8,128)(2,1)}, u32[]{:S(2)}, u32[]{:S(2)}) async-start(bf16[64,8,8192]{2,1,0:T(8,128)(2,1)} %fusion), calls=%async_computation | async-start | bytes 16777216 | tf_op jit(solution)/shard_map/all_to_all | solution.py:61
  55.2 7.8 %fusion.1 = bf16[64,8,8192]{2,1,0:T(8,128)(2,1)} fusion(bf16[256,8192]{1,0:T(8,128)(2,1)} %param.7, s32[256]{0:T(256)S(1)} %multiply_add_fusion.1), kind=kOutput, calls=%fused_computation.3 | convolution fusion | flops 2151809024 | bytes 12583936 | tf_op jit(solution)/shard_map/dot_general | solution.py:14
  63.0 178.0 %all-to-all-done = bf16[64,8,8192]{2,1,0:T(8,128)(2,1)} async-done(((bf16[64,8,8192]{2,1,0:T(8,128)(2,1)}), bf16[64,8,8192]{2,1,0:T(8,128)(2,1)}, u32[]{:S(2)}, u32[]{:S(2)}) %all-to-all-start) | async-done | bytes 8388640 | tf_op jit(solution)/shard_map/all_to_all | solution.py:61
  241.0 6.1 %all-to-all-start.2 = ((bf16[64,8,8192]{2,1,0:T(8,128)(2,1)}), bf16[64,8,8192]{2,1,0:T(8,128)(2,1)}, u32[]{:S(2)}, u32[]{:S(2)}) async-start(bf16[64,8,8192]{2,1,0:T(8,128)(2,1)} %fusion.1), calls=%async_computation.2 | async-start | bytes 16777216 | tf_op jit(solution)/shard_map/all_to_all | solution.py:60
  247.1 0.2 reduce-scatter.2.cloned.1.call-start
  247.3 1.7 copy.14
  249.0 183.8 %all-to-all-done.2 = bf16[64,8,8192]{2,1,0:T(8,128)(2,1)} async-done(((bf16[64,8,8192]{2,1,0:T(8,128)(2,1)}), bf16[64,8,8192]{2,1,0:T(8,128)(2,1)}, u32[]{:S(2)}, u32[]{:S(2)}) %all-to-all-start.2) | async-done | bytes 8388640 | tf_op jit(solution)/shard_map/all_to_all | solution.py:60
  432.8 11.3 %convolution_bitcast_fusion.1 = f32[1,1,64,8192]{3,2,1,0:T(8,128)} fusion(bf16[64,8,8192]{2,1,0:T(8,128)(2,1)} %all-to-all-done.2, bf16[64,8,8192]{2,1,0:T(8,128)(2,1)} %all-to-all-done, bf16[1,2,64,8192]{3,2,1,0:T(8,128)(2,1)S(1)} %bitcast.59), kind=kOutput, calls=%fused_computation.5 | convolution fusion | flops 1073774592 | bytes 19922944 | tf_op jit(solution)/shard_map/dot_general | solution.py:19
  444.1 11.3 %convolution_bitcast_fusion = f32[1,1,64,8192]{3,2,1,0:T(8,128)} fusion(bf16[64,8,8192]{2,1,0:T(8,128)(2,1)} %all-to-all-done, bf16[64,8,8192]{2,1,0:T(8,128)(2,1)} %all-to-all-done.2, bf16[1,2,64,8192]{3,2,1,0:T(8,128)(2,1)S(1)} %bitcast.60), kind=kOutput, calls=%fused_computation.4 | convolution fusion | flops 1073774592 | bytes 19922944 | tf_op jit(solution)/shard_map/dot_general | solution.py:22
  455.4 4.5 maximum_multiply_fusion
  460.0 0.0 copy-start.1
  460.0 0.0 copy-start.2
  460.0 0.0 reduce-scatter.2.cloned.1.call-update
  460.0 44.3 %reduce-scatter.2.cloned.1.call-done = f32[1,2,64,2048]{3,2,1,0:T(8,128)} async-done(((f32[1,2,64,8192]{3,2,1,0:T(8,128)}), f32[1,2,64,2048]{3,2,1,0:T(8,128)}) %reduce-scatter.2.cloned.1.call-update) | async-done | bytes 1048592 | tf_op jit(solution)/shard_map/reduce_scatter | solution.py:75
  504.3 0.0 copy-done.1
  504.3 0.0 copy-done.2
  504.3 3.3 add_divide_fusion
  (4 shorter events, 0.1 us)
Async XLA Ops:
  7.2 7.7 %copy-start.3 = (s32[256,1]{0,1:T(1,128)S(1)}, s32[256,1]{0,1:T(1,128)}, u32[]{:S(2)}) copy-start(s32[256,1]{0,1:T(1,128)} %param.9) | copy-start | bytes 3076
  7.2 7.7 %copy-start.4 = (s32[64]{0:T(128)S(1)}, s32[64]{0:T(128)}, u32[]{:S(2)}) copy-start(s32[64]{0:T(128)} %param.10) | copy-start | bytes 772
  9.8 29.6 %all-to-all-start.1 = ((bf16[4,1,2,64,2048]{4,3,2,1,0:T(8,128)(2,1)}), bf16[4,1,2,64,2048]{4,3,2,1,0:T(8,128)(2,1)S(1)}, u32[]{:S(2)}, u32[]{:S(2)}) async-start(bf16[4,1,2,64,2048]{4,3,2,1,0:T(8,128)(2,1)} %stack.16), calls=%async_computation.1 | async-start | bytes 4194304 | tf_op jit(solution)/shard_map/all_to_all | solution.py:64
  39.4 1.4 copy-start
  40.8 200.2 %all-to-all-start = ((bf16[64,8,8192]{2,1,0:T(8,128)(2,1)}), bf16[64,8,8192]{2,1,0:T(8,128)(2,1)}, u32[]{:S(2)}, u32[]{:S(2)}) async-start(bf16[64,8,8192]{2,1,0:T(8,128)(2,1)} %fusion), calls=%async_computation | async-start | bytes 16777216 | tf_op jit(solution)/shard_map/all_to_all | solution.py:61
  241.0 191.9 %all-to-all-start.2 = ((bf16[64,8,8192]{2,1,0:T(8,128)(2,1)}), bf16[64,8,8192]{2,1,0:T(8,128)(2,1)}, u32[]{:S(2)}, u32[]{:S(2)}) async-start(bf16[64,8,8192]{2,1,0:T(8,128)(2,1)} %fusion.1), calls=%async_computation.2 | async-start | bytes 16777216 | tf_op jit(solution)/shard_map/all_to_all | solution.py:60
  247.1 257.2 %reduce-scatter.2.cloned.1.call-start = ((), (), s32[]{:S(2)}) async-start(), calls=%async_computation.4 | async-start | bytes 5242880 | tf_op jit(solution)/shard_map/reduce_scatter | solution.py:75
  460.0 44.3 %copy-start.1 = (f32[1,2,64,2048]{3,2,1,0:T(8,128)S(1)}, f32[1,2,64,2048]{3,2,1,0:T(8,128)}, u32[]{:S(2)}) copy-start(f32[1,2,64,2048]{3,2,1,0:T(8,128)} %param.13) | copy-start | bytes 3145732
  460.0 44.3 %copy-start.2 = (f32[1,2,64,2048]{3,2,1,0:T(8,128)S(1)}, f32[1,2,64,2048]{3,2,1,0:T(8,128)}, u32[]{:S(2)}) copy-start(f32[1,2,64,2048]{3,2,1,0:T(8,128)} %param.12) | copy-start | bytes 3145732
Sparse Core Ops, SparseCore 0:
  460.1 44.1 reduce-scatter.1
